TPU v7x, 512 devices: a whole 4x8x8 slice. The times are simulated.
512 devices in a mesh: role: 4 (over x), ep: 64 (over z, y), dp: 2 (over core).
Axes of the slice: x: 4, y: 8, z: 8, core: 2. Of those that a mesh axis runs over, the one named last changes fastest.
Arguments:
- latents: bfloat16 [16, 4096, 1536], P(('role', 'dp'), 'ep'), may hold values from -6 to 6
- noise: bfloat16 [1, 16, 4096, 1536], P(None, ('role', 'dp'), 'ep'), may hold values from -6 to 6
- expert_ids: int32 [1, 16, 4096, 6], P(None, ('role', 'dp'), 'ep'), may hold values from 0 to 63, all different within a row; in each aligned block of 64 rows (0 to 63, 64 to 127, ..., all dimensions but the last counted through in order) at most 7 rows name the same one
- gate_values: float32 [1, 16, 4096, 6], P(None, ('role', 'dp'), 'ep'), may hold values from 0.1 to 1
- advantages: float32 [16], P(('role', 'dp')), may hold values from -4 to 4
- expert_pair: bfloat16 [64, 2, 768, 1536], P('ep', None, ('role', 'dp')), may hold values from -6 to 6
Outputs:
- final_latents: bfloat16 [16, 4096, 1536], P(('role', 'dp'), 'ep')
- new_down: bfloat16 [64, 768, 1536], P('ep')
Inputs may be any that keep to these rules, and one draw needn't show every extreme that they name: `expert_ids`: each row names 6 different experts. In every aligned block of 64 rows (steps, images and tokens taken together in order; one index of ep holds one block of an image at a step) no expert is named more than 7 times, a bound that some block reaches.
All inputs are finite; a program needn't handle non-finite values.
Results may differ from a plain program's by a relative error of at most 0.008.
Values may be sent and summed in bfloat16 or wider, within the bound.
A program may use at most 128 MiB of HBM per device.

v0:
```python
import math
import jax
import jax.numpy as jnp
from jax import lax
from jax.sharding import PartitionSpec as P

CAP = 7


def coefficients(section):
    moment = 0.95 - 0.4 * section
    noise_level = 0.3 * math.sqrt(moment / (1.0 - moment))
    factor = noise_level * noise_level / (2.0 * moment)
    keep_gain = 1.0 - 0.4 * factor
    drift_gain = -0.4 * (1.0 + factor * (1.0 - moment))
    noise_gain = noise_level * math.sqrt(0.4)
    return (keep_gain, drift_gain, noise_gain)


def slot_matrices(picked, weights, experts, capacity):
    image_count, tokens, chosen_count = picked.shape
    flat_ids = picked.reshape(image_count, tokens * chosen_count)
    onehot = (flat_ids[..., None] == jnp.arange(experts, dtype=jnp.int32)).astype(jnp.int32)
    ranks = jnp.cumsum(onehot, axis=1) - 1
    placed = jnp.sum(ranks * onehot, axis=2)
    image_column = jnp.arange(image_count, dtype=jnp.int32)[:, None]
    slot_ids = (flat_ids * image_count + image_column) * capacity + placed
    slot_ids = slot_ids.reshape(image_count * tokens, chosen_count)
    total_slots = experts * image_count * capacity
    marked = (slot_ids[..., None] == jnp.arange(total_slots, dtype=jnp.int32)).astype(jnp.float32)
    selected = jnp.sum(marked, axis=1)
    flat_weights = weights.reshape(image_count * tokens, chosen_count)
    slot_gate = jnp.sum(jnp.sum(marked * flat_weights[..., None], axis=1), axis=0)
    return (slot_ids, selected, slot_gate, flat_weights)


def expert_pass(inputs, w_up, w_down):
    width = inputs.shape[-1]
    hidden_units = w_up.shape[1]
    pre_act = jnp.einsum("jlcd,lhd->jlch", inputs, w_up, preferred_element_type=jnp.float32) * (
        1.0 / math.sqrt(width)
    )
    hidden = jax.nn.gelu(pre_act, approximate=True).astype(jnp.bfloat16)
    output = jnp.einsum("jlch,lhd->jlcd", hidden, w_down, preferred_element_type=jnp.float32) * (
        1.0 / math.sqrt(hidden_units)
    )
    returned = lax.all_to_all(
        output.astype(jnp.bfloat16), "ep", split_axis=0, concat_axis=0, tiled=True
    )
    return (returned, hidden)


def per_device(latents, noise, expert_ids, gate_values, advantages, expert_pair):
    ep_size = lax.axis_size("ep")
    group_size = lax.axis_size("role") * lax.axis_size("dp")
    local_experts = expert_pair.shape[0]
    experts = local_experts * ep_size
    capacity = CAP
    image_count = latents.shape[0]
    tok_count = latents.shape[1]
    width = latents.shape[2]
    top_count = expert_ids.shape[3]
    total_slots = experts * image_count * capacity
    full_pair = lax.all_gather(expert_pair, ("role", "dp"), axis=2, tiled=True)
    w_up = full_pair[:, 0]
    w_down = full_pair[:, 1]
    hidden_units = full_pair.shape[2]
    current = latents.reshape(image_count * tok_count, width)
    image_of_slot = jnp.arange(total_slots, dtype=jnp.int32) // capacity % image_count
    keep_gain, drift_gain, noise_gain = coefficients(0)
    slot_ids, selected, slot_gate, flat_weights = slot_matrices(
        expert_ids[0], gate_values[0], experts, capacity
    )
    selected_half = selected.astype(jnp.bfloat16)
    noise_now = noise[0].reshape(image_count * tok_count, width)
    slot_latent = jnp.einsum(
        "ts,td->sd", selected_half, current, preferred_element_type=jnp.float32
    )
    slot_latent = slot_latent.astype(jnp.bfloat16).reshape(
        ep_size, local_experts, image_count * capacity, width
    )
    slot_noise = jnp.einsum(
        "ts,td->sd", selected_half, noise_now, preferred_element_type=jnp.float32
    )
    image_factor = advantages * (drift_gain / noise_gain)
    slot_scale = slot_gate * image_factor[image_of_slot]
    home_cot = (
        (slot_scale[:, None] * slot_noise)
        .astype(jnp.bfloat16)
        .reshape(ep_size, local_experts, image_count * capacity, width)
    )
    returned, hidden = expert_pass(
        lax.all_to_all(slot_latent, "ep", split_axis=0, concat_axis=0, tiled=True), w_up, w_down
    )
    returned, hidden, cotangent = (
        returned,
        hidden,
        lax.all_to_all(home_cot, "ep", split_axis=0, concat_axis=0, tiled=True),
    )
    back_rows = returned.reshape(total_slots, width)
    taken = jnp.take(back_rows, slot_ids, axis=0)
    velocity = jnp.sum(flat_weights[..., None] * taken.astype(jnp.float32), axis=1)
    moved = (
        keep_gain * current.astype(jnp.float32)
        + drift_gain * velocity
        + noise_gain * noise_now.astype(jnp.float32)
    )
    current = moved.astype(jnp.bfloat16)
    kept_hidden = [hidden]
    kept_cot = [cotangent]
    rate = 10.0 / math.sqrt(tok_count * ep_size * top_count * image_count * group_size / experts)
    total = jnp.zeros((hidden_units, local_experts, width), jnp.float32)
    for hidden, cotangent in zip(kept_hidden, kept_cot):
        total = jnp.einsum("jlch,jlcd->hld", hidden, cotangent, preferred_element_type=jnp.float32)
    summed = lax.psum(
        (total * (1.0 / math.sqrt(hidden_units)))
        .reshape(hidden_units, local_experts * width)
        .astype(jnp.bfloat16),
        ("role", "dp"),
    ).astype(jnp.float32)
    summed = jnp.transpose(summed.reshape(hidden_units, local_experts, width), (1, 0, 2))
    new_down = (w_down.astype(jnp.float32) + rate * summed).astype(jnp.bfloat16)
    return (current.reshape(image_count, tok_count, width), new_down)


def solution(mesh):
    in_specs = (
        P(("role", "dp"), "ep", None),
        P(None, ("role", "dp"), "ep", None),
        P(None, ("role", "dp"), "ep", None),
        P(None, ("role", "dp"), "ep", None),
        P(("role", "dp")),
        P("ep", None, ("role", "dp"), None),
    )
    out_specs = (P(("role", "dp"), "ep", None), P("ep", None, None))
    return jax.shard_map(
        per_device, mesh=mesh, in_specs=in_specs, out_specs=out_specs, check_vma=False
    )
```

profile of v0, /device:TPU:8, one launch (start us, length us, event | category | flops | bytes accessed | tf_op | source)
XLA Modules:
  0.0 347.8 jit_solution(13016884792895209371)
XLA Ops:
  7.2 0.8 copy.62
  8.0 0.1 eq.44
  8.1 0.1 eq.40
  8.2 0.7 broadcast_multiply_fusion.1
  9.0 1.8 reduce-window.6
  10.8 0.1 slice.21
  10.9 0.1 copy.64
  11.0 0.1 fusion.26
  11.2 0.1 reduce_sum.45
  11.3 0.1 copy.67
  11.4 0.1 mul.180
  11.5 0.1 add.131
  11.6 0.8 mul.176
  12.3 0.6 compare_and_fusion
  12.9 0.6 select_reduce_fusion
  13.5 1.9 convolution_convert_fusion
  15.4 2.5 reshape.262
  17.9 16.9 %all-to-all-start = ((bf16[64,1,14,1536]{3,2,1,0:T(8,128)(2,1)}), bf16[64,1,14,1536]{3,2,1,0:T(8,128)(2,1)}, u32[]{:S(2)}, u32[]{:S(2)}) async-start(bf16[64,1,14,1536]{3,2,1,0:T(8,128)(2,1)} %bitcast.3), calls=%async_computation | async-start | bytes 6291456 | tf_op jit(solution)/shard_map/all_to_all | solution.py:93
  34.9 0.7 all-gather.2.cloned.1.call-update
  35.6 0.6 fusion.34
  36.2 1.3 fusion.30
  37.5 0.9 multiply_convert_fusion
  38.4 2.6 reshape.268
  41.0 73.6 %all-to-all-done = bf16[64,1,14,1536]{3,2,1,0:T(8,128)(2,1)} async-done(((bf16[64,1,14,1536]{3,2,1,0:T(8,128)(2,1)}), bf16[64,1,14,1536]{3,2,1,0:T(8,128)(2,1)}, u32[]{:S(2)}, u32[]{:S(2)}) %all-to-all-start) | async-done | bytes 2752544 | tf_op jit(solution)/shard_map/all_to_all | solution.py:93
  114.6 22.3 %all-to-all-start.2 = ((bf16[64,1,14,1536]{3,2,1,0:T(8,128)(2,1)}), bf16[64,1,14,1536]{3,2,1,0:T(8,128)(2,1)S(1)}, u32[]{:S(2)}, u32[]{:S(2)}) async-start(bf16[64,1,14,1536]{3,2,1,0:T(8,128)(2,1)} %bitcast.23), calls=%async_computation.2 | async-start | bytes 6291456 | tf_op jit(solution)/shard_map/all_to_all | solution.py:98
  136.9 8.1 %fusion.21 = bf16[64,14,768]{2,0,1:T(8,128)(2,1)S(1)} fusion(bf16[1,2,768,1536]{3,2,1,0:T(8,128)(2,1)} %all-gather.2.cloned.1.call-done, bf16[64,1,14,1536]{3,2,1,0:T(8,128)(2,1)} %all-to-all-done), kind=kOutput, calls=%fused_computation.31 | convolution fusion | flops 2120810496 | bytes 6881280 | tf_op jit(solution)/shard_map/jlcd,lhd->jlch/dot_general | solution.py:40
  145.0 2.3 fusion.1
  147.3 3.2 copy.71
  150.5 62.1 %all-to-all-done.2 = bf16[64,1,14,1536]{3,2,1,0:T(8,128)(2,1)S(1)} async-done(((bf16[64,1,14,1536]{3,2,1,0:T(8,128)(2,1)}), bf16[64,1,14,1536]{3,2,1,0:T(8,128)(2,1)S(1)}, u32[]{:S(2)}, u32[]{:S(2)}) %all-to-all-start.2) | async-done | bytes 2752544 | tf_op jit(solution)/shard_map/all_to_all | solution.py:98
  212.6 21.0 %all-to-all-start.1 = ((bf16[64,1,14,1536]{3,2,1,0:T(8,128)(2,1)}), bf16[64,1,14,1536]{3,2,1,0:T(8,128)(2,1)}, u32[]{:S(2)}, u32[]{:S(2)}) async-start(bf16[64,1,14,1536]{3,2,1,0:T(8,128)(2,1)} %copy.71), calls=%async_computation.1 | async-start | bytes 6291456 | tf_op jit(solution)/shard_map/all_to_all | solution.py:47
  233.6 0.3 all-reduce.2.cloned.1.call-start
  233.9 7.0 %fusion.2 = bf16[768,1536]{1,0:T(8,128)(2,1)} fusion(bf16[64,14,768]{2,0,1:T(8,128)(2,1)} %copy-done.5, bf16[64,1,14,1536]{3,2,1,0:T(8,128)(2,1)S(1)} %all-to-all-done.2), kind=kOutput, calls=%fused_computation.10 | convolution fusion | flops 2116288512 | bytes 6488064 | tf_op jit(solution)/shard_map/jlch,jlcd->hld/dot_general | solution.py:114
  240.9 0.1 reduce_sum.47
  241.1 0.1 mul.198
  241.2 0.7 copy.61
  241.9 0.1 copy.72
  242.0 0.7 compare_select_fusion.1
  242.7 0.1 copy.73
  242.8 0.1 reshape.272
  242.9 0.8 copy.68
  243.7 76.6 %all-reduce.2.cloned.1.call-done = bf16[768,1536]{1,0:T(8,128)(2,1)} async-done(((bf16[768,1536]{1,0:T(8,128)(2,1)}), bf16[768,1536]{1,0:T(8,128)(2,1)}) %all-reduce.2.cloned.1.call-update) | async-done | bytes 2359312 | tf_op jit(solution)/shard_map/psum | solution.py:115
  320.3 4.5 %fusion.16 = bf16[1,768,1536]{2,1,0:T(8,128)(2,1)} fusion(bf16[768,1536]{1,0:T(8,128)(2,1)} %all-reduce.2.cloned.1.call-done, bf16[1,2,768,1536]{3,2,1,0:T(8,128)(2,1)} %all-gather.2.cloned.1.call-done), kind=kLoop, calls=%fused_computation.27 | loop fusion | flops 5898240 | bytes 7077888 | tf_op jit(solution)/shard_map/convert_element_type | solution.py:122
  324.8 3.8 %reshape.267 = bf16[896,1536]{1,0:T(8,128)(2,1)S(1)} reshape(bf16[64,1,14,1536]{3,2,1,0:T(8,128)(2,1)} %all-to-all-done.1) | data formatting | bytes 5505024 | tf_op jit(solution)/shard_map/reshape | solution.py:100
  328.6 3.8 %gather_fusion = bf16[768,1536]{1,0:T(8,128)(2,1)} fusion(bf16[896,1536]{1,0:T(8,128)(2,1)S(1)} %reshape.267, s32[1024]{0:T(1024)S(1)} %pad_clamp_fusion), kind=kCustom, calls=%fused_computation | custom fusion | bytes 4721664 | tf_op jit(solution)/shard_map/jit(_take)/gather | solution.py:101
  332.4 3.5 %reshape.271 = bf16[128,6,1536]{2,1,0:T(8,128)(2,1)S(1)} reshape(bf16[768,1536]{1,0:T(8,128)(2,1)} %gather_fusion) | data formatting | bytes 4718592 | tf_op jit(solution)/shard_map/jit(_take)/gather | solution.py:101
  336.0 4.0 %multiply_reduce_fusion = f32[128,1536]{1,0:T(8,128)S(1)} fusion(bf16[128,6,1536]{2,1,0:T(8,128)(2,1)S(1)} %reshape.271, f32[128,6]{1,0:T(8,128)} %copy.61, pred[128,6]{1,0:T(8,128)(4,1)S(1)} %copy.68), kind=kLoop, calls=%fused_computation.1 | loop fusion | flops 4521984 | bytes 3149568 | tf_op jit(solution)/shard_map/reduce_sum | solution.py:102
  340.0 0.1 broadcast_multiply_fusion
  340.1 0.9 fusion.24
  (24 shorter events, 0.2 us)
Async XLA Ops:
  11.6 6.4 %copy-start.3 = (s32[128]{0:T(128)}, s32[128]{0:T(128)S(1)}, u32[]{:S(2)}) copy-start(s32[128]{0:T(128)S(1)} %add.131) | copy-start | bytes 1540
  17.9 17.6 %copy-start.4 = (f32[2]{0:T(128)S(1)}, f32[2]{0:T(128)}, u32[]{:S(2)}) copy-start(f32[2]{0:T(128)} %param.10) | copy-start | bytes 28
  17.9 19.6 %copy-start = (bf16[1,2,64,1536]{3,2,1,0:T(8,128)(2,1)S(1)}, bf16[1,2,64,1536]{3,2,1,0:T(8,128)(2,1)}, u32[]{:S(2)}) copy-start(bf16[1,2,64,1536]{3,2,1,0:T(8,128)(2,1)} %param.7) | copy-start | bytes 1179652
  17.9 96.6 %all-to-all-start = ((bf16[64,1,14,1536]{3,2,1,0:T(8,128)(2,1)}), bf16[64,1,14,1536]{3,2,1,0:T(8,128)(2,1)}, u32[]{:S(2)}, u32[]{:S(2)}) async-start(bf16[64,1,14,1536]{3,2,1,0:T(8,128)(2,1)} %bitcast.3), calls=%async_computation | async-start | bytes 6291456 | tf_op jit(solution)/shard_map/all_to_all | solution.py:93
  34.8 102.1 %all-gather.2.cloned.1.call-start = ((), (), s32[]{:S(2)}) async-start(), calls=%async_computation.3 | async-start | bytes 5308416 | tf_op jit(solution)/shard_map/all_gather | solution.py:64
  114.6 98.0 %all-to-all-start.2 = ((bf16[64,1,14,1536]{3,2,1,0:T(8,128)(2,1)}), bf16[64,1,14,1536]{3,2,1,0:T(8,128)(2,1)S(1)}, u32[]{:S(2)}, u32[]{:S(2)}) async-start(bf16[64,1,14,1536]{3,2,1,0:T(8,128)(2,1)} %bitcast.23), calls=%async_computation.2 | async-start | bytes 6291456 | tf_op jit(solution)/shard_map/all_to_all | solution.py:98
  136.9 8.1 %copy-start.2 = (bf16[1,2,768,1536]{3,2,1,0:T(8,128)(2,1)S(1)}, bf16[1,2,768,1536]{3,2,1,0:T(8,128)(2,1)}, u32[]{:S(2)}) copy-start(bf16[1,2,768,1536]{3,2,1,0:T(8,128)(2,1)} %all-gather.2.cloned.1.call-done) | copy-start | bytes 14155780
  145.0 2.3 copy-start.5
  212.6 112.2 %all-to-all-start.1 = ((bf16[64,1,14,1536]{3,2,1,0:T(8,128)(2,1)}), bf16[64,1,14,1536]{3,2,1,0:T(8,128)(2,1)}, u32[]{:S(2)}, u32[]{:S(2)}) async-start(bf16[64,1,14,1536]{3,2,1,0:T(8,128)(2,1)} %copy.71), calls=%async_computation.1 | async-start | bytes 6291456 | tf_op jit(solution)/shard_map/all_to_all | solution.py:47
  233.6 86.7 %all-reduce.2.cloned.1.call-start = ((), (), s32[]{:S(2)}) async-start(), calls=%async_computation.4 | async-start | bytes 4718592 | tf_op jit(solution)/shard_map/psum | solution.py:115
  336.0 4.1 %copy-start.1 = (bf16[2,64,1536]{2,1,0:T(8,128)(2,1)S(1)}, bf16[2,64,1536]{2,1,0:T(8,128)(2,1)}, u32[]{:S(2)}) copy-start(bf16[2,64,1536]{2,1,0:T(8,128)(2,1)} %param.6) | copy-start | bytes 1179652
Sparse Core Ops, SparseCore 0:
  37.8 40.3 all-gather.1
  241.1 79.2 all-reduce.1
where the time goes:
time: 349 us; the launch traced here: 348 us
  waiting for transfers between devices  213 us (61%)
  starting transfers between devices  60.5 us (17%)
  local copies, waits for them, and re-layouts  24.5 us (7%)
  matrix products  20.2 us (6%)
  other arithmetic  15.4 us (4%)
  between operations  14.3 us (4%)
    psum x1, waiting for transfers between devices, per_device(): lax.psum((total * (1.0 / math.sqrt(hidden_units))).reshape(hidden_units,...  76.6 us
    all_to_all x1, waiting for transfers between devices, per_device(): lax.all_to_all(slot_latent, 'ep', split_axis=0, concat_axis=0, tiled=True)  73.6 us
    all_to_all x1, waiting for transfers between devices, per_device(): lax.all_to_all(home_cot, 'ep', split_axis=0, concat_axis=0, tiled=True)  62.1 us
    all_to_all x1, starting transfers between devices, per_device(): lax.all_to_all(home_cot, 'ep', split_axis=0, concat_axis=0, tiled=True)  22.3 us
    all_to_all x1, starting transfers between devices, expert_pass(): lax.all_to_all(output.astype(jnp.bfloat16), 'ep', split_axis=0, concat_ax...  21 us
    all_to_all x1, starting transfers between devices, per_device(): lax.all_to_all(slot_latent, 'ep', split_axis=0, concat_axis=0, tiled=True)  16.9 us
    dot_general x1, matrix products, expert_pass(): jnp.einsum('jlcd,lhd->jlch', inputs, w_up, preferred_element_type=jnp.flo...  8.06 us
    gather x2, local copies, waits for them, and re-layouts, per_device(): taken = jnp.take(back_rows, slot_ids, axis=0)  7.35 us
  transfers between devices with their start and end apart: 5, of which 3 were waited for; matrix products, arithmetic and copies ran while one was open for 10% of the time, Pallas kernels for 0%

commit v1 on v0

--- a/solution.py
+++ b/solution.py
@@ -113,10 +113,13 @@
     for hidden, cotangent in zip(kept_hidden, kept_cot):
         total = jnp.einsum("jlch,jlcd->hld", hidden, cotangent, preferred_element_type=jnp.float32)
     summed = lax.psum(
-        (total * (1.0 / math.sqrt(hidden_units)))
-        .reshape(hidden_units, local_experts * width)
-        .astype(jnp.bfloat16),
-        ("role", "dp"),
+        lax.psum(
+            (total * (1.0 / math.sqrt(hidden_units)))
+            .reshape(hidden_units, local_experts * width)
+            .astype(jnp.bfloat16),
+            "dp",
+        ),
+        "role",
     ).astype(jnp.float32)
     summed = jnp.transpose(summed.reshape(hidden_units, local_experts, width), (1, 0, 2))
     new_down = (w_down.astype(jnp.float32) + rate * summed).astype(jnp.bfloat16)

time: 349 us -> 386 us (1.11)
  the two profiles are of different devices: /device:TPU:8 before, /device:TPU:1 now
where the time goes in v1:
time: 386 us; the launch traced here: 385 us
  waiting for transfers between devices  246 us (64%)
  starting transfers between devices  66.5 us (17%)
  local copies, waits for them, and re-layouts  23.9 us (6%)
  matrix products  20.2 us (5%)
  other arithmetic  14.7 us (4%)
  between operations  14 us (4%)
    psum x1, waiting for transfers between devices, per_device(): lax.psum(lax.psum((total * (1.0 / math.sqrt(hidden_units))).reshape(hidde...  74.6 us
    all_to_all x1, waiting for transfers between devices, per_device(): lax.all_to_all(slot_latent, 'ep', split_axis=0, concat_axis=0, tiled=True)  67 us
    all_to_all x1, waiting for transfers between devices, per_device(): lax.all_to_all(home_cot, 'ep', split_axis=0, concat_axis=0, tiled=True)  61.7 us
    psum x1, waiting for transfers between devices, per_device(): lax.psum((total * (1.0 / math.sqrt(hidden_units))).reshape(hidden_units,...  41.9 us
    all_to_all x1, starting transfers between devices, per_device(): lax.all_to_all(home_cot, 'ep', split_axis=0, concat_axis=0, tiled=True)  27.8 us
    all_to_all x1, starting transfers between devices, expert_pass(): lax.all_to_all(output.astype(jnp.bfloat16), 'ep', split_axis=0, concat_ax...  20.9 us
    all_to_all x1, starting transfers between devices, per_device(): lax.all_to_all(slot_latent, 'ep', split_axis=0, concat_axis=0, tiled=True)  17.5 us
    dot_general x1, matrix products, expert_pass(): jnp.einsum('jlcd,lhd->jlch', inputs, w_up, preferred_element_type=jnp.flo...  8.06 us
  transfers between devices with their start and end apart: 6, of which 4 were waited for; matrix products, arithmetic and copies ran while one was open for 8% of the time, Pallas kernels for 0%

profile of v1, /device:TPU:1, one launch (start us, length us, event | category | flops | bytes accessed | tf_op | source)
XLA Modules:
  0.0 385.1 jit_solution(14806151401202601418)
XLA Ops:
  7.2 0.8 copy.62
  8.0 0.1 eq.44
  8.1 0.1 eq.40
  8.2 0.7 broadcast_multiply_fusion.1
  9.0 1.8 reduce-window.6
  10.8 0.1 slice.21
  10.9 0.1 copy.64
  11.0 0.1 fusion.26
  11.2 0.1 reduce_sum.45
  11.3 0.1 copy.67
  11.4 0.1 mul.180
  11.5 0.1 add.133
  11.6 0.8 mul.176
  12.3 0.5 compare_and_fusion
  12.9 0.6 select_reduce_fusion
  13.5 1.9 convolution_convert_fusion
  15.4 2.5 reshape.262
  17.9 17.5 %all-to-all-start = ((bf16[64,1,14,1536]{3,2,1,0:T(8,128)(2,1)}), bf16[64,1,14,1536]{3,2,1,0:T(8,128)(2,1)}, u32[]{:S(2)}, u32[]{:S(2)}) async-start(bf16[64,1,14,1536]{3,2,1,0:T(8,128)(2,1)} %bitcast.3), calls=%async_computation | async-start | bytes 6291456 | tf_op jit(solution)/shard_map/all_to_all | solution.py:93
  35.4 0.7 all-gather.2.cloned.1.call-update
  36.2 0.6 fusion.34
  36.7 1.3 fusion.30
  38.1 0.9 multiply_convert_fusion
  39.0 2.6 reshape.268
  41.6 67.0 %all-to-all-done = bf16[64,1,14,1536]{3,2,1,0:T(8,128)(2,1)} async-done(((bf16[64,1,14,1536]{3,2,1,0:T(8,128)(2,1)}), bf16[64,1,14,1536]{3,2,1,0:T(8,128)(2,1)}, u32[]{:S(2)}, u32[]{:S(2)}) %all-to-all-start) | async-done | bytes 2752544 | tf_op jit(solution)/shard_map/all_to_all | solution.py:93
  108.6 27.8 %all-to-all-start.2 = ((bf16[64,1,14,1536]{3,2,1,0:T(8,128)(2,1)}), bf16[64,1,14,1536]{3,2,1,0:T(8,128)(2,1)S(1)}, u32[]{:S(2)}, u32[]{:S(2)}) async-start(bf16[64,1,14,1536]{3,2,1,0:T(8,128)(2,1)} %bitcast.23), calls=%async_computation.2 | async-start | bytes 6291456 | tf_op jit(solution)/shard_map/all_to_all | solution.py:98
  136.5 8.1 %fusion.21 = bf16[64,14,768]{2,0,1:T(8,128)(2,1)S(1)} fusion(bf16[1,2,768,1536]{3,2,1,0:T(8,128)(2,1)} %all-gather.2.cloned.1.call-done, bf16[64,1,14,1536]{3,2,1,0:T(8,128)(2,1)} %all-to-all-done), kind=kOutput, calls=%fused_computation.31 | convolution fusion | flops 2120810496 | bytes 6881280 | tf_op jit(solution)/shard_map/jlcd,lhd->jlch/dot_general | solution.py:40
  144.5 2.3 fusion.1
  146.8 3.2 copy.71
  150.0 61.7 %all-to-all-done.2 = bf16[64,1,14,1536]{3,2,1,0:T(8,128)(2,1)S(1)} async-done(((bf16[64,1,14,1536]{3,2,1,0:T(8,128)(2,1)}), bf16[64,1,14,1536]{3,2,1,0:T(8,128)(2,1)S(1)}, u32[]{:S(2)}, u32[]{:S(2)}) %all-to-all-start.2) | async-done | bytes 2752544 | tf_op jit(solution)/shard_map/all_to_all | solution.py:98
  211.7 20.9 %all-to-all-start.1 = ((bf16[64,1,14,1536]{3,2,1,0:T(8,128)(2,1)}), bf16[64,1,14,1536]{3,2,1,0:T(8,128)(2,1)}, u32[]{:S(2)}, u32[]{:S(2)}) async-start(bf16[64,1,14,1536]{3,2,1,0:T(8,128)(2,1)} %copy.71), calls=%async_computation.1 | async-start | bytes 6291456 | tf_op jit(solution)/shard_map/all_to_all | solution.py:47
  232.7 7.0 %fusion.2 = bf16[768,1536]{1,0:T(8,128)(2,1)} fusion(bf16[64,14,768]{2,0,1:T(8,128)(2,1)} %copy-done.7, bf16[64,1,14,1536]{3,2,1,0:T(8,128)(2,1)S(1)} %all-to-all-done.2), kind=kOutput, calls=%fused_computation.10 | convolution fusion | flops 2116288512 | bytes 6488064 | tf_op jit(solution)/shard_map/jlch,jlcd->hld/dot_general | solution.py:114
  239.7 0.3 all-reduce.5.cloned.1.call-start
  240.0 41.9 %all-reduce.3.cloned.1.call-done = bf16[768,1536]{1,0:T(8,128)(2,1)} async-done(((bf16[768,1536]{1,0:T(8,128)(2,1)}), bf16[768,1536]{1,0:T(8,128)(2,1)}) %all-reduce.3.cloned.1.call-update) | async-done | bytes 2359312 | tf_op jit(solution)/shard_map/psum | solution.py:116
  281.9 0.1 reduce_sum.47
  282.0 0.1 mul.198
  282.1 0.7 copy.61
  282.8 0.1 copy.72
  282.9 0.1 copy.73
  283.1 0.1 reshape.272
  283.2 0.1 copy.68
  283.4 74.6 %all-reduce.5.cloned.1.call-done = bf16[768,1536]{1,0:T(8,128)(2,1)} async-done(((bf16[768,1536]{1,0:T(8,128)(2,1)}), bf16[768,1536]{1,0:T(8,128)(2,1)}) %all-reduce.5.cloned.1.call-update) | async-done | bytes 2359312 | tf_op jit(solution)/shard_map/psum | solution.py:115
  357.9 4.5 %fusion.16 = bf16[1,768,1536]{2,1,0:T(8,128)(2,1)} fusion(bf16[768,1536]{1,0:T(8,128)(2,1)} %all-reduce.5.cloned.1.call-done, bf16[1,2,768,1536]{3,2,1,0:T(8,128)(2,1)} %all-gather.2.cloned.1.call-done), kind=kLoop, calls=%fused_computation.27 | loop fusion | flops 5898240 | bytes 7077888 | tf_op jit(solution)/shard_map/convert_element_type | solution.py:125
  362.4 3.8 reshape.267
  366.2 3.8 gather_fusion
  370.0 3.5 reshape.271
  373.6 4.0 %multiply_reduce_fusion = f32[128,1536]{1,0:T(8,128)S(1)} fusion(bf16[128,6,1536]{2,1,0:T(8,128)(2,1)S(1)} %reshape.271, f32[128,6]{1,0:T(8,128)} %copy.61, pred[128,6]{1,0:T(8,128)(4,1)S(1)} %copy.68), kind=kLoop, calls=%fused_computation.1 | loop fusion | flops 4521984 | bytes 3149568 | tf_op jit(solution)/shard_map/reduce_sum | solution.py:102
  377.6 0.1 broadcast_multiply_fusion
  377.7 0.9 fusion.24
  (31 shorter events, 0.2 us)
Async XLA Ops:
  11.6 6.3 %copy-start.4 = (s32[128]{0:T(128)}, s32[128]{0:T(128)S(1)}, u32[]{:S(2)}) copy-start(s32[128]{0:T(128)S(1)} %add.133) | copy-start | bytes 1540
  17.9 18.3 %copy-start.6 = (f32[2]{0:T(128)S(1)}, f32[2]{0:T(128)}, u32[]{:S(2)}) copy-start(f32[2]{0:T(128)} %param.10) | copy-start | bytes 28
  17.9 20.2 %copy-start = (bf16[1,2,64,1536]{3,2,1,0:T(8,128)(2,1)S(1)}, bf16[1,2,64,1536]{3,2,1,0:T(8,128)(2,1)}, u32[]{:S(2)}) copy-start(bf16[1,2,64,1536]{3,2,1,0:T(8,128)(2,1)} %param.7) | copy-start | bytes 1179652
  17.9 90.7 %all-to-all-start = ((bf16[64,1,14,1536]{3,2,1,0:T(8,128)(2,1)}), bf16[64,1,14,1536]{3,2,1,0:T(8,128)(2,1)}, u32[]{:S(2)}, u32[]{:S(2)}) async-start(bf16[64,1,14,1536]{3,2,1,0:T(8,128)(2,1)} %bitcast.3), calls=%async_computation | async-start | bytes 6291456 | tf_op jit(solution)/shard_map/all_to_all | solution.py:93
  35.4 101.0 %all-gather.2.cloned.1.call-start = ((), (), s32[]{:S(2)}) async-start(), calls=%async_computation.3 | async-start | bytes 5308416 | tf_op jit(solution)/shard_map/all_gather | solution.py:64
  108.6 103.1 %all-to-all-start.2 = ((bf16[64,1,14,1536]{3,2,1,0:T(8,128)(2,1)}), bf16[64,1,14,1536]{3,2,1,0:T(8,128)(2,1)S(1)}, u32[]{:S(2)}, u32[]{:S(2)}) async-start(bf16[64,1,14,1536]{3,2,1,0:T(8,128)(2,1)} %bitcast.23), calls=%async_computation.2 | async-start | bytes 6291456 | tf_op jit(solution)/shard_map/all_to_all | solution.py:98
  136.4 8.1 %copy-start.2 = (bf16[1,2,768,1536]{3,2,1,0:T(8,128)(2,1)S(1)}, bf16[1,2,768,1536]{3,2,1,0:T(8,128)(2,1)}, u32[]{:S(2)}) copy-start(bf16[1,2,768,1536]{3,2,1,0:T(8,128)(2,1)} %all-gather.2.cloned.1.call-done) | copy-start | bytes 14155780
  144.5 2.3 copy-start.7
  211.7 150.7 %all-to-all-start.1 = ((bf16[64,1,14,1536]{3,2,1,0:T(8,128)(2,1)}), bf16[64,1,14,1536]{3,2,1,0:T(8,128)(2,1)}, u32[]{:S(2)}, u32[]{:S(2)}) async-start(bf16[64,1,14,1536]{3,2,1,0:T(8,128)(2,1)} %copy.71), calls=%async_computation.1 | async-start | bytes 6291456 | tf_op jit(solution)/shard_map/all_to_all | solution.py:47
  232.6 49.2 %all-reduce.3.cloned.1.call-start = ((), (), s32[]{:S(2)}) async-start(), calls=%async_computation.4 | async-start | bytes 4718592 | tf_op jit(solution)/shard_map/psum | solution.py:116
  239.7 43.2 %copy-start.5 = (s32[128]{0:T(128)S(1)}, s32[128]{0:T(128)}, u32[]{:S(2)}) copy-start(s32[128]{0:T(128)} %copy-done.4) | copy-start | bytes 1540
  239.7 43.5 %copy-start.3 = (pred[128,6]{0,1:T(8,128)(4,1)S(1)}, pred[128,6]{0,1:T(8,128)(4,1)}, u32[]{:S(2)}) copy-start(pred[128,6]{0,1:T(8,128)(4,1)} %get-tuple-element.4) | copy-start | bytes 2308
  239.7 118.2 %all-reduce.5.cloned.1.call-start = ((), (), s32[]{:S(2)}) async-start(), calls=%async_computation.5 | async-start | bytes 4718592 | tf_op jit(solution)/shard_map/psum | solution.py:115
  373.6 4.1 %copy-start.1 = (bf16[2,64,1536]{2,1,0:T(8,128)(2,1)S(1)}, bf16[2,64,1536]{2,1,0:T(8,128)(2,1)}, u32[]{:S(2)}) copy-start(bf16[2,64,1536]{2,1,0:T(8,128)(2,1)} %param.6) | copy-start | bytes 1179652
Sparse Core Ops, SparseCore 0:
  38.4 41.0 all-gather.1
  239.8 41.9 all-reduce.2
  284.3 73.5 all-reduce.4
